TPU v7x, 512 devices: a whole 4x8x8 slice. The times are simulated.
512 devices in a mesh: dp: 32 (over z_lo, y, core), ctx: 16 (over z_hi, x).
Axes of the slice: x: 4, y: 8, z: 8 (z_hi: 4, z_lo: 2; z = z_hi * 2 + z_lo), core: 2. Of those that a mesh axis runs over, the one named last changes fastest.
Arguments:
- tokens: bfloat16 [32, 4096, 3072], P('dp', 'ctx'), may hold values from -6 to 6
- queries: bfloat16 [32, 4096, 2048], P('dp', 'ctx'), may hold values from -6 to 6
- master: float32 [3072, 2048], P(('dp', 'ctx')), may hold values from -0.5051815 to 0.5051815
- grad: float32 [3072, 2048], P(('dp', 'ctx')), may hold values from -6 to 6
- moment: float32 [3072, 2048], P(('dp', 'ctx')), may hold values from -4 to 4
- second: float32 [3072, 2048], P(('dp', 'ctx')), may hold values from 0.05 to 4
Outputs:
- new_master: float32 [3072, 2048], P(('dp', 'ctx'))
- new_moment: float32 [3072, 2048], P(('dp', 'ctx'))
- new_second: float32 [3072, 2048], P(('dp', 'ctx'))
- codes: bfloat16 [3072, 2048], P(('dp', 'ctx'))
- attended: bfloat16 [32, 4096, 2048], P('dp', 'ctx')
All inputs are finite; a program needn't handle non-finite values. Where the computation divides by a largest or mean magnitude, that divisor is 1e-20 or more.
Results may differ from a plain program's by a relative error of at most 0.0091.
Values may be sent and summed in bfloat16 or wider, within the bound.
A program may use at most 128 MiB of HBM per device.

v0:
```python
import jax
import jax.numpy as jnp
from jax import lax
from jax.sharding import PartitionSpec as P

HD = 128
KVH = 8
WINDOW = 512
GROUP = 2


beta_one = 0.9
beta_two = 0.95
adam_eps = 1e-08
decay_rate = 0.1
learn_rate = 0.001
step_count = 1000
score_scale = 1.0 / 12.0
soft_cap = 50.0
rope_base = 10000.0


def passed_along(block, axis, distance):
    devices = range(lax.axis_size(axis))
    route = [(i - distance, i) for i in devices if i - distance in devices]
    return lax.ppermute(block, axis, route)


def adamw(master, grad, moment, second):
    new_moment = beta_one * moment + (1.0 - beta_one) * grad
    new_second = beta_two * second + (1.0 - beta_two) * grad * grad
    moment_hat = new_moment / (1.0 - beta_one**step_count)
    second_hat = new_second / (1.0 - beta_two**step_count)
    update = moment_hat / (jnp.sqrt(second_hat) + adam_eps) + decay_rate * master
    return (master - learn_rate * update, new_moment, new_second)


def rotate_keys(product, peak, positions):
    scaled = product * peak[None, :]
    half = HD // 2
    keys = scaled[:, : KVH * HD].reshape(-1, KVH, HD)
    values = scaled[:, KVH * HD :]
    freqs = rope_base ** (-jnp.arange(half, dtype=jnp.float32) * 2.0 / HD)
    angles = positions.astype(jnp.float32)[:, None] * freqs[None, :]
    cosine = jnp.cos(angles)[:, None, :]
    sine = jnp.sin(angles)[:, None, :]
    lower = keys[..., :half]
    upper = keys[..., half:]
    turned = jnp.concatenate(
        [lower * cosine - upper * sine, upper * cosine + lower * sine], axis=-1
    )
    turned = turned.reshape(-1, KVH * HD)
    return jnp.concatenate([turned, values], axis=1).astype(jnp.bfloat16)


def attend(query_rows, key_rows, query_start, key_start):
    rows = query_rows.shape[0]
    span = key_rows.shape[0]
    qpos = query_start + jnp.arange(rows, dtype=jnp.int32)
    kpos = key_start + jnp.arange(span, dtype=jnp.int32)
    gap = qpos[:, None] - kpos[None, :]
    valid = (gap >= 0) & (gap < WINDOW) & (kpos[None, :] >= 0)
    grouped = query_rows.reshape(rows, KVH, GROUP * HD).transpose(1, 0, 2)
    keys = key_rows[:, : KVH * HD].reshape(span, KVH, HD).transpose(1, 0, 2)
    values = key_rows[:, KVH * HD :].reshape(span, KVH, HD).transpose(1, 0, 2)

    def one_head(triple):
        query_head, key_head, value_head = triple
        query_head = query_head.reshape(rows, GROUP, HD)
        scores = (
            jnp.einsum("rgd,sd->grs", query_head, key_head, preferred_element_type=jnp.float32)
            * score_scale
        )
        capped = soft_cap * jnp.tanh(scores / soft_cap)
        weights = jnp.where(valid[None], jnp.exp(capped), jnp.zeros_like(capped))
        probs = (weights / jnp.sum(weights, axis=-1, keepdims=True)).astype(jnp.bfloat16)
        mixed = jnp.einsum("grs,sd->rgd", probs, value_head, preferred_element_type=jnp.float32)
        return mixed.astype(jnp.bfloat16)

    heads = lax.map(one_head, (grouped, keys, values))
    return heads.transpose(1, 0, 2, 3).reshape(rows, KVH * GROUP * HD)


def on_device(tokens, queries, master, grad, moment, second):
    new_master, new_moment, new_second = adamw(master, grad, moment, second)
    local_peak = jnp.max(jnp.abs(new_master), axis=0)
    peak = lax.pmax(local_peak, ("dp", "ctx")) + 1e-06
    codes = (new_master / peak[None, :]).astype(jnp.bfloat16)
    rows = tokens[0]
    count = rows.shape[0]
    empty = jnp.zeros((count, codes.shape[1]), jnp.float32)
    piece = lax.all_gather(codes, ("dp", "ctx"), axis=0, tiled=True)
    columns = lax.slice_in_dim(rows, 0, piece.shape[0], axis=1)
    product = empty + jnp.dot(columns, piece, preferred_element_type=jnp.float32)
    query_start = lax.axis_index("ctx") * count
    positions = query_start + jnp.arange(count, dtype=jnp.int32)
    keyval = rotate_keys(product, peak, positions)
    shards_back = WINDOW // count
    earlier = []
    piece = keyval
    for back in range(shards_back):
        piece = passed_along(piece, "ctx", 1)
        earlier.insert(0, piece)
    key_rows = jnp.concatenate(earlier + [keyval], axis=0)
    attended = attend(queries[0], key_rows, query_start, query_start - shards_back * count)
    return (new_master, new_moment, new_second, codes, attended[None])


def solution(mesh):
    return jax.shard_map(
        on_device,
        mesh=mesh,
        in_specs=(
            P("dp", "ctx", None),
            P("dp", "ctx", None),
            P(("dp", "ctx"), None),
            P(("dp", "ctx"), None),
            P(("dp", "ctx"), None),
            P(("dp", "ctx"), None),
        ),
        out_specs=(
            P(("dp", "ctx"), None),
            P(("dp", "ctx"), None),
            P(("dp", "ctx"), None),
            P(("dp", "ctx"), None),
            P("dp", "ctx", None),
        ),
        check_vma=False,
    )
```

profile of v0, /device:TPU:256, one launch (start us, length us, event | category | flops | bytes accessed | tf_op | source)
XLA Modules:
  0.0 1736.4 jit_solution(11675856337357749930)
XLA Ops:
  7.2 1.7 abs_reduce_fusion
  9.0 97.7 %pmax.7 = f32[2048]{0:T(1024)S(1)} all-reduce(f32[2048]{0:T(1024)S(1)} %get-tuple-element.120), channel_id=1, replica_groups=mesh['dp'=32,'ctx'=16] {'dp','ctx'}, use_global_device_ids=true, to_apply=%region_1.0 | all-reduce | flops 2048 | bytes 16384 | tf_op jit(solution)/shard_map/pmax | solution.py:87
  107.7 1432.2 %all-gather.3.cloned.1.call-done = bf16[512,6,2048]{2,1,0:T(8,128)(2,1)} async-done(((bf16[1,6,2048]{2,1,0:T(8,128)(2,1)}), bf16[512,6,2048]{2,1,0:T(8,128)(2,1)}) %all-gather.3.cloned.1.call-update) | async-done | bytes 12582928 | tf_op jit(solution)/shard_map/all_gather | solution.py:92
  1540.0 20.6 %reshape.106 = bf16[3072,2048]{1,0:T(8,128)(2,1)} reshape(bf16[512,6,2048]{2,1,0:T(8,128)(2,1)} %all-gather.3.cloned.1.call-done) | data formatting | bytes 25165824
  1560.6 6.6 fusion.14
  1567.5 3.9 collective-permute-start
  1571.5 32.4 %collective-permute-done = bf16[256,2048]{0,1:T(8,128)(2,1)} collective-permute-done((bf16[256,2048]{0,1:T(8,128)(2,1)S(1)}, bf16[256,2048]{0,1:T(8,128)(2,1)}, u32[]{:S(2)}, u32[]{:S(2)}) %collective-permute-start) | collective-permute-done | bytes 1048608 | tf_op jit(solution)/shard_map/ppermute | solution.py:26
  1603.9 1.9 collective-permute-start.1
  1605.8 2.3 copy.22
  1608.7 67.3 %collective-permute-done.1 = bf16[256,2048]{0,1:T(8,128)(2,1)} collective-permute-done((bf16[256,2048]{0,1:T(8,128)(2,1)}, bf16[256,2048]{0,1:T(8,128)(2,1)}, u32[]{:S(2)}, u32[]{:S(2)}) %collective-permute-start.1) | collective-permute-done | bytes 1048608 | tf_op jit(solution)/shard_map/ppermute | solution.py:26
  1676.1 10.6 maximum_maximum_fusion
  1686.7 1.4 fusion.19
  1688.0 1.6 copy.21
  1689.6 37.7 %while.13 = (s32[]{:T(128)}, bf16[8,256,2,128]{1,3,2,0:T(8,128)(2,1)}, bf16[8,768,128]{1,2,0:T(8,128)(2,1)}, bf16[8,768,128]{2,1,0:T(8,128)(2,1)}, bf16[8,256,25...) while((s32[]{:T(128)}, ...), condition=%wide.region_4.5_spmd.clone, body=%wide.region_2.4_spmd.clone.sunk | while | flops 204342528 | bytes 6035809 | solution.py:80
  1689.6 0.9 constant_dynamic-slice_fusion.2
  1690.8 1.5 bitcast_select_fusion.2
  1692.3 2.0 fusion.35
  1695.5 1.5 bitcast_select_fusion.2
  1697.0 2.0 fusion.35
  1700.2 1.5 bitcast_select_fusion.2
  1701.7 2.0 fusion.35
  1704.9 1.5 bitcast_select_fusion.2
  1706.4 2.0 fusion.35
  1709.6 1.5 bitcast_select_fusion.2
  1711.1 2.0 fusion.35
  1714.3 1.5 bitcast_select_fusion.2
  1715.8 2.0 fusion.35
  1719.0 1.5 bitcast_select_fusion.2
  1720.6 2.0 fusion.35
  1723.8 1.5 bitcast_select_fusion.2
  1725.3 2.0 fusion.35
  1727.3 2.3 copy.26
  (35 shorter events, 10.6 us)
Async XLA Ops:
  7.2 1553.4 %copy-start = (bf16[1,256,3072]{2,1,0:T(8,128)(2,1)S(1)}, bf16[1,256,3072]{2,1,0:T(8,128)(2,1)}, u32[]{:S(2)}) copy-start(bf16[1,256,3072]{2,1,0:T(8,128)(2,1)} %param.8) | copy-start | bytes 4718596
  7.2 1532.8 %all-gather.3.cloned.1.call-start = ((), (), s32[]{:S(2)}) async-start(), calls=%async_computation | async-start | bytes 16809984 | tf_op jit(solution)/shard_map/all_gather | solution.py:92
  9.0 1599.1 %copy-start.1 = (f32[6,2048]{1,0:T(8,128)}, f32[6,2048]{1,0:T(8,128)S(1)}, u32[]{:S(2)}) copy-start(f32[6,2048]{1,0:T(8,128)S(1)} %get-tuple-element.121) | copy-start | bytes 147460
  1567.5 36.4 %collective-permute-start = (bf16[256,2048]{0,1:T(8,128)(2,1)S(1)}, bf16[256,2048]{0,1:T(8,128)(2,1)}, u32[]{:S(2)}, u32[]{:S(2)}) collective-permute-start(bf16[256,2048]{0,1:T(8,128)(2,1)S(1)} %pad_maximum_fusion), channel_id=1, source_target_pairs={{0,1},{1,2},{2,3},{3,4},{4,5},{5,6},{6,7},{7,8},{8,9},{9,10},{10,1... | collective-permute-start | bytes 3145736 | tf_op jit(solution)/shard_map/ppermute | solution.py:26
  1603.9 72.2 %collective-permute-start.1 = (bf16[256,2048]{0,1:T(8,128)(2,1)}, bf16[256,2048]{0,1:T(8,128)(2,1)}, u32[]{:S(2)}, u32[]{:S(2)}) collective-permute-start(bf16[256,2048]{0,1:T(8,128)(2,1)} %collective-permute-done), channel_id=1, source_target_pairs={{0,1},{1,2},{2,3},{3,4},{4,5},{5,6},{6,7},{7,8},{8,9},{9,10},{10,1... | collective-permute-start | bytes 3145736 | tf_op jit(solution)/shard_map/ppermute | solution.py:26
Sparse Core Ops, SparseCore 0:
  107.5 1432.4 all-gather.2
where the time goes:
time: 1740 us
  waiting for transfers between devices  1530 us (88%)
  blocking collectives  97.7 us (6%)
  local copies, waits for them, and re-layouts  35.5 us (2%)
  matrix products  34.6 us (2%)
    all_gather x1, waiting for transfers between devices, on_device(): piece = lax.all_gather(codes, ('dp', 'ctx'), axis=0, tiled=True)  1430 us
    ppermute x2, waiting for transfers between devices, passed_along(): return lax.ppermute(block, axis, route)  99.8 us
    pmax x1, blocking collectives, on_device(): peak = lax.pmax(local_peak, ('dp', 'ctx')) + 1e-06  97.7 us
  transfers between devices with their start and end apart: 3, of which 3 were waited for; matrix products, arithmetic and copies ran while one was open for 0% of the time, Pallas kernels for 0%

commit v1 on v0

v1 whole, which is shorter than its diff:
```python
import functools

import jax
import jax.numpy as jnp
from jax import lax
from jax.experimental import pallas as pl
from jax.experimental.pallas import tpu as pltpu
from jax.sharding import PartitionSpec as P

HD = 128
KVH = 8
WINDOW = 512
GROUP = 2
ROWS = 256
WIDTH = 3072
KVW = 2048

beta_one = 0.9
beta_two = 0.95
adam_eps = 1e-08
decay_rate = 0.1
learn_rate = 0.001
step_count = 1000
soft_cap = 50.0
rope_base = 10000.0

MESH = pl.DeviceIdType.MESH
HEADS = 4
LOG2E = 1.4426950408889634


def rem(a, b):
    return lax.rem(a, jnp.int32(b))


def div(a, b):
    return lax.div(a, jnp.int32(b))


def kernel(
    tok_hbm, q_hbm, master, grad, moment, second, cosine, sine,
    attended, new_master, new_moment, new_second, codes,
    weights, tok, qs, keyval, sent_out, staged, pieces, block, peaks,
    tok_sem, q_sem, piece_sem, x_send, x_recv, first_send, first_recv,
    ring_send, ring_recv, halo_send, halo_recv, out_send, out_recv, peak_sem,
):
    dp, ctx = lax.axis_index("dp"), lax.axis_index("ctx")
    core, y, z_lo = rem(dp, 2), rem(div(dp, 2), 8), div(dp, 16)
    x, z_hi = rem(ctx, 4), div(ctx, 4)
    z = 2 * z_hi + z_lo
    kind, half = div(z_hi, 2), rem(z_hi, 2)
    row_group = (z_lo * 8 + y) * 2

    def device(xx, yy, zz):
        return ((rem(zz, 2) * 8 + yy) * 2 + core, div(zz, 2) * 4 + xx)

    sibling = (row_group + 1 - core, ctx)
    barrier = pltpu.get_barrier_semaphore()

    def greet(i, _):
        to_core, to_ctx = rem(i, 2), div(i, 2)

        @pl.when((to_core != core) | (to_ctx != ctx))
        def _():
            pl.semaphore_signal(
                barrier, inc=1, device_id=(row_group + to_core, to_ctx), device_id_type=MESH
            )

        return 0

    lax.fori_loop(0, 32, greet, 0)

    def greet_y(k, _):
        pl.semaphore_signal(
            barrier, inc=1, device_id=device(x, rem(y + k, 8), z), device_id_type=MESH
        )
        return 0

    lax.fori_loop(1, 8, greet_y, 0)

    def greet_z(k, _):
        pl.semaphore_signal(
            barrier, inc=1, device_id=device(x, y, rem(z + 2 * k + 1, 8)), device_id_type=MESH
        )
        return 0

    lax.fori_loop(0, 4, greet_z, 0)

    own_cols = pl.ds(pl.multiple_of(core * 1024, 1024), 1024)
    their_cols = pl.ds(pl.multiple_of((1 - core) * 1024, 1024), 1024)
    own_tok = pltpu.make_async_copy(tok_hbm, tok.at[0], tok_sem.at[0])
    own_q = pltpu.make_async_copy(q_hbm.at[:, own_cols], qs.at[0], q_sem.at[0])
    own_tok.start()
    own_q.start()

    g = grad[...]
    old = master[...]
    mom = beta_one * moment[...] + (1.0 - beta_one) * g
    sec = beta_two * second[...] + (1.0 - beta_two) * g * g
    mom_hat = mom / (1.0 - beta_one**step_count)
    sec_hat = sec / (1.0 - beta_two**step_count)
    update = mom_hat / (jnp.sqrt(sec_hat) + adam_eps) + decay_rate * old
    fresh = old - learn_rate * update
    new_master[...] = fresh
    new_moment[...] = mom
    new_second[...] = sec
    staged[...] = jnp.zeros_like(staged)
    for b in range(16):
        staged[b, 0:6, :] = fresh[:, 128 * b : 128 * b + 128]

    pl.semaphore_wait(barrier, 42)

    def owner(b):
        head = rem(b, 8)
        return div(head, 4), (div(b, 8) * 2 + core) * 4 + rem(head, 4)

    def send_piece(b, _):
        to_core, to_ctx = owner(b)
        mine = (to_core == core) & (to_ctx == ctx)

        @pl.when(mine)
        def _():
            pltpu.make_async_copy(staged.at[b], pieces.at[ctx], piece_sem.at[1]).start()

        @pl.when(jnp.logical_not(mine))
        def _():
            pltpu.make_async_remote_copy(
                src_ref=staged.at[b],
                dst_ref=pieces.at[ctx],
                send_sem=piece_sem.at[0],
                recv_sem=piece_sem.at[1],
                device_id=(row_group + to_core, to_ctx),
                device_id_type=MESH,
            ).start()

        return 0

    lax.fori_loop(0, 16, send_piece, 0)
    pltpu.make_async_copy(pieces, pieces, piece_sem.at[1]).wait()

    for j in range(16):
        block[6 * j : 6 * j + 6, :] = pieces[j, 0:6, :]
    weights[x, kind, z_lo, y, half] = block[...].astype(jnp.bfloat16)

    def x_copy(k):
        ref = weights.at[x, kind, z_lo, y, half]
        return pltpu.make_async_remote_copy(
            src_ref=ref, dst_ref=ref, send_sem=x_send.at[k], recv_sem=x_recv.at[k],
            device_id=device(rem(x + k + 1, 4), y, z), device_id_type=MESH,
        )

    for k in range(3):
        x_copy(k).start()

    their_tok = pltpu.make_async_remote_copy(
        src_ref=tok_hbm, dst_ref=tok.at[1], send_sem=tok_sem.at[1], recv_sem=tok_sem.at[2],
        device_id=sibling, device_id_type=MESH,
    )
    their_q = pltpu.make_async_remote_copy(
        src_ref=q_hbm.at[:, their_cols], dst_ref=qs.at[1], send_sem=q_sem.at[1],
        recv_sem=q_sem.at[2], device_id=sibling, device_id_type=MESH,
    )
    their_tok.start()
    their_q.start()

    for k in range(3):
        ref = weights.at[rem(x + 3 - k, 4), kind, z_lo, y, half]
        pltpu.make_async_copy(ref, ref, x_recv.at[k]).wait()

    def first(h, _):
        upper = weights.at[h, kind, z_lo, y, half, pl.ds(0, 48), :]
        lower = weights.at[h, kind, z_lo, y, half, pl.ds(48, 48), :]

        def to_peer(k, _):
            pltpu.make_async_remote_copy(
                src_ref=upper, dst_ref=upper, send_sem=first_send.at[0, h],
                recv_sem=first_recv.at[0, h],
                device_id=device(x, rem(y + k, 8), z), device_id_type=MESH,
            ).start()
            pltpu.make_async_remote_copy(
                src_ref=lower, dst_ref=lower, send_sem=first_send.at[1, h],
                recv_sem=first_recv.at[1, h],
                device_id=device(x, y, rem(z + k, 8)), device_id_type=MESH,
            ).start()
            return 0

        lax.fori_loop(1, 8, to_peer, 0)
        return 0

    lax.fori_loop(0, HEADS, first, 0)

    def wait_first(sems, h):
        for axis in range(2):
            ref = weights.at[h, 0, 0, pl.ds(0, 7), 0, pl.ds(0, 48), :]
            pltpu.make_async_copy(ref, ref, sems.at[axis, h]).wait()

    def part(axis, h, at, which):
        if axis == 0:
            rows = (pl.ds(0, 8), pl.ds(0, 4), pl.ds(4, 4))[which]
            return weights.at[
                h, div(at, 4), rem(at, 2), rows, rem(div(at, 2), 2), pl.ds(0, 48), :
            ]
        kinds = (pl.ds(0, 2), pl.ds(0, 1), pl.ds(1, 1))[which]
        return weights.at[h, kinds, :, at, :, pl.ds(48, 48), :]

    def ring_copy(axis, way, h, step, received):
        here = (z, y)[axis]
        sign = 1 - 2 * way
        origin = rem(here - sign * (step + (1 if received else 0)) + 16, 8)
        which = 0 if step < 3 else 1 + way
        target = rem(here + sign + 8, 8)
        ref = part(axis, h, origin, which)
        return pltpu.make_async_remote_copy(
            src_ref=ref, dst_ref=ref, send_sem=ring_send.at[axis, way, h, step],
            recv_sem=ring_recv.at[axis, way, h, step],
            device_id=device(x, y, target) if axis == 0 else device(x, target, z),
            device_id_type=MESH,
        )

    def ring_start(h, step):
        for axis in range(2):
            for way in range(2):
                ring_copy(axis, way, h, step, False).start()

    def ring_wait(h, step):
        for axis in range(2):
            for way in range(2):
                ring_copy(axis, way, h, step, True).wait_recv()

    def project(h):
        total = jnp.zeros((2 * ROWS, 2 * HD), jnp.float32)
        top = jnp.zeros((8, 2 * HD), jnp.float32)
        for c in range(4):
            low = weights[h, 0, c // 2, 4 * (c % 2) : 4 * (c % 2) + 4].reshape(768, HD)
            high = weights[h, 1, c // 2, 4 * (c % 2) : 4 * (c % 2) + 4].reshape(768, HD)
            both = jnp.concatenate([low, high], axis=1)
            rows = tok[:, :, 768 * c : 768 * c + 768].reshape(2 * ROWS, 768)
            total = total + jnp.dot(rows, both, preferred_element_type=jnp.float32)
            size = jnp.abs(both.astype(jnp.float32)).reshape(96, 8, 2 * HD)
            top = jnp.maximum(top, jnp.max(size, axis=0))
        top = jnp.broadcast_to(jnp.max(top, axis=0, keepdims=True), (8, 2 * HD))
        peaks[core, h, 0] = top[:, :HD]
        peaks[core, h, 1] = top[:, HD:]
        keys = total[:, :HD]
        turned = pltpu.roll(keys, 64, 1)
        for s in range(2):
            span = slice(ROWS * s, ROWS * s + ROWS)
            rotated = keys[span] * cosine[...] + turned[span] * sine[...]
            keyval[h, s, 0, 512:768, :] = rotated.astype(jnp.bfloat16)
            keyval[h, s, 1, 512:768, :] = total[span, HD:].astype(jnp.bfloat16)

    next_ctx = (dp, rem(ctx + 1, 16))

    def halo_copy(h, hop):
        src = keyval.at[h, :, :, pl.ds(512 - 256 * hop, 256), :]
        dst = keyval.at[h, :, :, pl.ds(256 - 256 * hop, 256), :]
        return pltpu.make_async_remote_copy(
            src_ref=src, dst_ref=dst, send_sem=halo_send.at[hop, h],
            recv_sem=halo_recv.at[hop, h], device_id=next_ctx, device_id_type=MESH,
        )

    row_id = lax.broadcasted_iota(jnp.int32, (2 * 128, 128), 0)
    row_id = jnp.where(row_id >= 128, row_id - 128, row_id)
    col_id = lax.broadcasted_iota(jnp.int32, (2 * 128, 128), 1)
    past = col_id > row_id

    def attend(h):
        def one(i, _):
            s, a = div(i, 2), rem(i, 2)
            start = pl.multiple_of(a * 128, 128)
            cols = pl.ds(pl.multiple_of(h * 256, 256), 256)
            q = qs[s, pl.ds(start, 128), cols]
            q = jnp.concatenate([q[:, :HD], q[:, HD:]], axis=0)
            keys = keyval[h, s, 0, pl.ds(start, 640), :]
            values = keyval[h, s, 1, pl.ds(start, 640), :]
            scores = lax.dot_general(
                q, keys, (((1,), (1,)), ((), ())), preferred_element_type=jnp.float32
            )
            weight = jnp.exp2(jnp.tanh(scores * (1.0 / 600.0)) * (soft_cap * LOG2E))
            tiles = []
            for t in range(5):
                tile = weight[:, 128 * t : 128 * t + 128]
                inside = (128 * t - 512 + ctx * 256 + start) >= 0
                if t == 0:
                    tile = jnp.where(past & inside, tile, 0.0)
                elif t == 4:
                    tile = jnp.where(past, 0.0, tile)
                else:
                    tile = jnp.where(inside, tile, 0.0)
                tiles.append(tile)
            norm = jnp.sum(tiles[0] + tiles[1] + tiles[2] + tiles[3] + tiles[4], axis=1, keepdims=True)
            weight = jnp.concatenate([t.astype(jnp.bfloat16) for t in tiles], axis=1)
            mixed = jnp.dot(weight, values, preferred_element_type=jnp.float32)
            mixed = (mixed / norm).astype(jnp.bfloat16)
            mixed = jnp.concatenate([mixed[:128], mixed[128:]], axis=1)

            @pl.when(s == 0)
            def _():
                out_cols = pl.ds(pl.multiple_of(core * 1024 + h * 256, 256), 256)
                attended[pl.ds(start, 128), out_cols] = mixed

            @pl.when(s == 1)
            def _():
                sent_out[h, pl.ds(start, 128), :] = mixed

            return 0

        lax.fori_loop(0, 4, one, 0)

    def out_copy(h):
        out_cols = pl.ds(pl.multiple_of(core * 1024 + h * 256, 256), 256)
        return pltpu.make_async_remote_copy(
            src_ref=sent_out.at[h], dst_ref=attended.at[:, out_cols],
            send_sem=out_send.at[h], recv_sem=out_recv.at[h],
            device_id=sibling, device_id_type=MESH,
        )

    own_tok.wait()
    own_q.wait()
    their_tok.wait()
    their_q.wait()

    def turn(t, _):
        @pl.when(t < 4)
        def _():
            wait_first(first_recv, t)
            ring_start(t, 0)

        @pl.when((t >= 1) & (t < 5))
        def _():
            ring_wait(t - 1, 1)
            ring_start(t - 1, 2)

        @pl.when((t >= 2) & (t < 6))
        def _():
            ring_wait(t - 2, 3)
            project(t - 2)
            halo_copy(t - 2, 0).start()

        @pl.when(t < 4)
        def _():
            ring_wait(t, 0)
            ring_start(t, 1)

        @pl.when((t >= 1) & (t < 5))
        def _():
            ring_wait(t - 1, 2)
            ring_start(t - 1, 3)

        @pl.when((t >= 3) & (t < 7))
        def _():
            halo_copy(t - 3, 0).wait_recv()
            halo_copy(t - 3, 1).start()

        @pl.when(t >= 4)
        def _():
            halo_copy(t - 4, 1).wait_recv()
            attend(t - 4)
            out_copy(t - 4).start()

        return 0

    lax.fori_loop(0, 8, turn, 0)

    peak_copy = pltpu.make_async_remote_copy(
        src_ref=peaks.at[core], dst_ref=peaks.at[core], send_sem=peak_sem.at[0],
        recv_sem=peak_sem.at[1], device_id=sibling, device_id_type=MESH,
    )
    peak_copy.start()

    @pl.when(half == core)
    def _():
        ref = staged.at[pl.ds(0, 15)]
        pltpu.make_async_copy(ref, ref, piece_sem.at[0]).wait()

    @pl.when(half != core)
    def _():
        pltpu.make_async_copy(staged, staged, piece_sem.at[0]).wait()

    for k in range(3):
        x_copy(k).wait_send()

    def drain(h, _):
        wait_first(first_send, h)
        for step in range(4):
            for axis in range(2):
                for way in range(2):
                    ring_copy(axis, way, h, step, False).wait_send()
        halo_copy(h, 0).wait_send()
        halo_copy(h, 1).wait_send()
        out_copy(h).wait_send()
        theirs = pl.ds(pl.multiple_of((1 - core) * 1024 + h * 256, 256), 256)
        ref = attended.at[:, theirs]
        pltpu.make_async_copy(ref, ref, out_recv.at[h]).wait()
        return 0

    lax.fori_loop(0, HEADS, drain, 0)

    peak_copy.wait_send()
    ref = peaks.at[1 - core]
    pltpu.make_async_copy(ref, ref, peak_sem.at[1]).wait()
    for b in range(16):
        head = b % 8
        peak = peaks[head // 4, head % 4, b // 8, 0:1, :] + 1e-06
        codes[:, 128 * b : 128 * b + 128] = (staged[b, 0:6, :] / peak).astype(jnp.bfloat16)


def on_device(tokens, queries, master, grad, moment, second):
    query_start = lax.axis_index("ctx") * ROWS
    positions = query_start + jnp.arange(ROWS, dtype=jnp.int32)
    freqs = rope_base ** (-jnp.arange(HD // 2, dtype=jnp.float32) * 2.0 / HD)
    angles = positions.astype(jnp.float32)[:, None] * freqs[None, :]
    cosine, sine = jnp.cos(angles), jnp.sin(angles)
    cosine = jnp.concatenate([cosine, cosine], axis=1)
    sine = jnp.concatenate([-sine, sine], axis=1)
    vmem = pl.BlockSpec(memory_space=pltpu.VMEM)
    hbm = pl.BlockSpec(memory_space=pl.ANY)
    dma = pltpu.SemaphoreType.DMA
    f32, bf16 = jnp.float32, jnp.bfloat16
    attended, new_master, new_moment, new_second, codes = pl.pallas_call(
        kernel,
        out_shape=(
            jax.ShapeDtypeStruct((ROWS, KVW), bf16),
            jax.ShapeDtypeStruct((6, KVW), f32),
            jax.ShapeDtypeStruct((6, KVW), f32),
            jax.ShapeDtypeStruct((6, KVW), f32),
            jax.ShapeDtypeStruct((6, KVW), bf16),
        ),
        in_specs=[hbm, hbm] + [vmem] * 6,
        out_specs=(vmem,) * 5,
        scratch_shapes=[
            pltpu.VMEM((HEADS, 2, 2, 8, 2, 96, HD), bf16),
            pltpu.VMEM((2, ROWS, WIDTH), bf16),
            pltpu.VMEM((2, ROWS, 1024), bf16),
            pltpu.VMEM((HEADS, 2, 2, 768, HD), bf16),
            pltpu.VMEM((HEADS, ROWS, 256), bf16),
            pltpu.VMEM((16, 8, 128), f32),
            pltpu.VMEM((16, 8, 128), f32),
            pltpu.VMEM((96, 128), f32),
            pltpu.VMEM((2, HEADS, 2, 8, 128), f32),
            dma((3,)),
            dma((3,)),
            dma((2,)),
            dma((3,)),
            dma((3,)),
            dma((2, HEADS)),
            dma((2, HEADS)),
            dma((2, 2, HEADS, 4)),
            dma((2, 2, HEADS, 4)),
            dma((2, HEADS)),
            dma((2, HEADS)),
            dma((HEADS,)),
            dma((HEADS,)),
            dma((2,)),
        ],
        compiler_params=pltpu.CompilerParams(
            collective_id=0, has_side_effects=True, vmem_limit_bytes=40 * 1024 * 1024
        ),
    )(tokens[0], queries[0], master, grad, moment, second, cosine, sine)
    return (new_master, new_moment, new_second, codes, attended[None])


def solution(mesh):
    rows = P(("dp", "ctx"), None)
    return jax.shard_map(
        on_device,
        mesh=mesh,
        in_specs=(P("dp", "ctx", None), P("dp", "ctx", None), rows, rows, rows, rows),
        out_specs=(rows, rows, rows, rows, P("dp", "ctx", None)),
        check_vma=False,
    )
```

time: 1740 us -> 172 us (0.10)
  the two profiles are of different devices: /device:TPU:256 before, /device:TPU:65 now
where the time goes in v1:
time: 172 us; the launch traced here: 171 us
  Pallas kernels  161 us (94%)
  local copies, waits for them, and re-layouts  8.74 us (5%)
    pallas_call x1, Pallas kernels, on_device(): pl.pallas_call(kernel, out_shape=(jax.ShapeDtypeStruct((ROWS, KVW), bf16)...  161 us
    unnamed x17, local copies, waits for them, and re-layouts  8.74 us

profile of v1, /device:TPU:65, one launch (start us, length us, event | category | flops | bytes accessed | tf_op | source)
XLA Modules:
  0.0 171.5 jit_solution(1957415017083667358)
XLA Ops:
  0.6 0.0 copy-start.1
  0.7 0.5 fusion
  1.2 0.1 pad_maximum_fusion
  1.4 0.5 copy-done.1
  1.9 0.0 copy-start
  1.9 1.4 copy-done
  3.3 0.0 copy-start.2
  3.3 0.8 copy-done.2
  4.1 0.0 copy-start.3
  4.1 0.8 copy-done.3
  4.9 0.0 copy-start.4
  4.9 0.8 copy-done.4
  5.8 0.0 copy-start.5
  5.8 0.8 copy-done.5
  6.6 161.4 %shard_map.101 = (bf16[256,2048]{1,0:T(8,128)(2,1)S(1)}, f32[6,2048]{1,0:T(8,128)S(1)}, f32[6,2048]{1,0:T(8,128)S(1)}, f32[6,2048]{1,0:T(8,128)S(1)}, bf16[6,2048]{1,0:T(8,128)(2,1)S(1)}) custom-call(bf16[256,3072]{1,0:T(8,128)(2,1)S(1)} %bitcast.3, bf16[256,2048]{1,0:T(8,128)(2,1)S(1)} %bitcast.4, f32[6,2048]{1,0:T(8,128)S(1)} %copy-done.2, ...), custom_call_target="tpu_custom_call" | custom-call | tf_op jit(solution)/shard_map/pallas_call | solution.py:420
  168.0 0.6 copy.16
  168.6 0.6 copy.17
  169.3 0.6 copy.18
  169.9 0.6 copy.19
  170.5 1.0 copy.20
  (2 shorter events, 0.0 us)
Async XLA Ops:
  0.6 1.2 copy-start.1
  1.9 1.4 copy-start
  3.3 0.8 copy-start.2
  4.1 0.8 copy-start.3
  4.9 0.8 copy-start.4
  5.8 0.8 copy-start.5

commit v2 on v1

--- a/solution.py
+++ b/solution.py
@@ -29,6 +29,19 @@
 LOG2E = 1.4426950408889634
 
 
+PROJECT, LATE, ATTEND, START = 4, 5, 6, 7
+
+
+def listed(text):
+    kinds = {"0": 0, "1": 1, "2": 2, "3": 3, "P": PROJECT, "L": LATE, "A": ATTEND, "S": START}
+    return [4 * kinds[item[0]] + int(item[1]) for item in text.split()]
+
+
+ORDER = listed("S0 S1 00 S2") + listed("01 S3 10 11") + listed("20 02 21 30")
+ORDER += listed("12 31 P0 03") + listed("22 13 P1 L0") + listed("32 23 P2 L1")
+ORDER += listed("33 A0 P3 L2") + listed("A1 L3 A2 A3")
+
+
 def rem(a, b):
     return lax.rem(a, jnp.int32(b))
 
@@ -38,11 +51,12 @@
 
 
 def kernel(
-    tok_hbm, q_hbm, master, grad, moment, second, cosine, sine,
+    tok_hbm, q_hbm, master_hbm, grad_hbm, moment_hbm, second_hbm, cosine, sine,
     attended, new_master, new_moment, new_second, codes,
-    weights, tok, qs, keyval, sent_out, staged, pieces, block, peaks,
-    tok_sem, q_sem, piece_sem, x_send, x_recv, first_send, first_recv,
-    ring_send, ring_recv, halo_send, halo_recv, out_send, out_recv, peak_sem,
+    weights, tok, qs, keyval, relay, detour, sent_out, state, staged, pieces, block, peaks,
+    tok_sem, q_sem, state_sem, piece_sem, x_send, x_recv, first_send, first_recv,
+    ring_send, ring_recv, early_send, late_send, near_recv, far_recv, relay_recv, detour_recv,
+    out_send, out_recv, peak_sem,
 ):
     dp, ctx = lax.axis_index("dp"), lax.axis_index("ctx")
     core, y, z_lo = rem(dp, 2), rem(div(dp, 2), 8), div(dp, 16)
@@ -55,6 +69,12 @@
         return ((rem(zz, 2) * 8 + yy) * 2 + core, div(zz, 2) * 4 + xx)
 
     sibling = (row_group + 1 - core, ctx)
+    loads = [
+        pltpu.make_async_copy(ref, state.at[i], state_sem.at[i])
+        for i, ref in enumerate((master_hbm, grad_hbm, moment_hbm, second_hbm))
+    ]
+    for load in loads:
+        load.start()
     barrier = pltpu.get_barrier_semaphore()
 
     def greet(i, _):
@@ -93,10 +113,11 @@
     own_tok.start()
     own_q.start()
 
-    g = grad[...]
-    old = master[...]
-    mom = beta_one * moment[...] + (1.0 - beta_one) * g
-    sec = beta_two * second[...] + (1.0 - beta_two) * g * g
+    for load in loads:
+        load.wait()
+    old, g = state[0], state[1]
+    mom = beta_one * state[2] + (1.0 - beta_one) * g
+    sec = beta_two * state[3] + (1.0 - beta_two) * g * g
     mom_hat = mom / (1.0 - beta_one**step_count)
     sec_hat = sec / (1.0 - beta_two**step_count)
     update = mom_hat / (jnp.sqrt(sec_hat) + adam_eps) + decay_rate * old
@@ -167,7 +188,7 @@
         ref = weights.at[rem(x + 3 - k, 4), kind, z_lo, y, half]
         pltpu.make_async_copy(ref, ref, x_recv.at[k]).wait()
 
-    def first(h, _):
+    def first(h):
         upper = weights.at[h, kind, z_lo, y, half, pl.ds(0, 48), :]
         lower = weights.at[h, kind, z_lo, y, half, pl.ds(48, 48), :]
 
@@ -185,9 +206,6 @@
             return 0
 
         lax.fori_loop(1, 8, to_peer, 0)
-        return 0
-
-    lax.fori_loop(0, HEADS, first, 0)
 
     def wait_first(sems, h):
         for axis in range(2):
@@ -203,11 +221,11 @@
         kinds = (pl.ds(0, 2), pl.ds(0, 1), pl.ds(1, 1))[which]
         return weights.at[h, kinds, :, at, :, pl.ds(48, 48), :]
 
-    def ring_copy(axis, way, h, step, received):
+    def ring_copy(axis, way, h, step, received, last):
         here = (z, y)[axis]
         sign = 1 - 2 * way
         origin = rem(here - sign * (step + (1 if received else 0)) + 16, 8)
-        which = 0 if step < 3 else 1 + way
+        which = 1 + way if last else 0
         target = rem(here + sign + 8, 8)
         ref = part(axis, h, origin, which)
         return pltpu.make_async_remote_copy(
@@ -217,15 +235,15 @@
             device_id_type=MESH,
         )
 
-    def ring_start(h, step):
+    def ring_start(h, step, last):
         for axis in range(2):
             for way in range(2):
-                ring_copy(axis, way, h, step, False).start()
-
-    def ring_wait(h, step):
+                ring_copy(axis, way, h, step, False, last).start()
+
+    def ring_wait(h, step, last):
         for axis in range(2):
             for way in range(2):
-                ring_copy(axis, way, h, step, True).wait_recv()
+                ring_copy(axis, way, h, step, True, last).wait_recv()
 
     def project(h):
         total = jnp.zeros((2 * ROWS, 2 * HD), jnp.float32)
@@ -249,15 +267,115 @@
             keyval[h, s, 0, 512:768, :] = rotated.astype(jnp.bfloat16)
             keyval[h, s, 1, 512:768, :] = total[span, HD:].astype(jnp.bfloat16)
 
-    next_ctx = (dp, rem(ctx + 1, 16))
-
-    def halo_copy(h, hop):
-        src = keyval.at[h, :, :, pl.ds(512 - 256 * hop, 256), :]
-        dst = keyval.at[h, :, :, pl.ds(256 - 256 * hop, 256), :]
-        return pltpu.make_async_remote_copy(
-            src_ref=src, dst_ref=dst, send_sem=halo_send.at[hop, h],
-            recv_sem=halo_recv.at[hop, h], device_id=next_ctx, device_id_type=MESH,
-        )
+    def slot(h, s, n):
+        return keyval.at[h, s, :, pl.ds(256 * n, 256), :]
+
+    def place(xx, up):
+        return (dp, rem(z_hi + up, 4) * 4 + xx)
+
+    def send(src, dst, send_sem, recv_sem, to):
+        pltpu.make_async_remote_copy(
+            src_ref=src, dst_ref=dst, send_sem=send_sem, recv_sem=recv_sem,
+            device_id=to, device_id_type=MESH,
+        ).start()
+
+    def near(src, h, s, sem, to):
+        send(src, slot(h, s, 1), sem, near_recv.at[h, s], to)
+
+    def far(src, h, s, sem, to):
+        send(src, slot(h, s, 0), sem, far_recv.at[h, s], to)
+
+    def early(h):
+        sem = early_send.at[h]
+
+        @pl.when(x == 3)
+        def _():
+            send(slot(h, 0, 2), relay.at[h], sem, relay_recv.at[h], place(3, 1))
+            send(slot(h, 1, 2), relay.at[h], sem, relay_recv.at[h], place(0, 0))
+
+        @pl.when(x == 2)
+        def _():
+            far(slot(h, 0, 2), h, 0, sem, place(0, 1))
+            send(slot(h, 1, 2), relay.at[h], sem, relay_recv.at[h], place(1, 0))
+
+        @pl.when(x < 3)
+        def _():
+            for s in range(2):
+                near(slot(h, s, 2), h, s, sem, place(x + 1, 0))
+
+        @pl.when(x == 1)
+        def _():
+            for s in range(2):
+                far(slot(h, s, 2), h, s, sem, place(3, 0))
+
+        @pl.when(x == 0)
+        def _():
+            send(slot(h, 1, 2), detour.at[h], sem, detour_recv.at[h], place(3, 0))
+
+    def wait_slot(sems, h, s, n):
+        pltpu.make_async_copy(slot(h, s, n), slot(h, s, n), sems.at[h, s]).wait()
+
+    def late(h):
+        sem = late_send.at[h]
+
+        @pl.when(x != 2)
+        def _():
+            pltpu.make_async_copy(relay.at[h], relay.at[h], relay_recv.at[h]).wait()
+
+        @pl.when(x == 0)
+        def _():
+            near(relay.at[h], h, 1, sem, place(0, 1))
+
+        @pl.when(x == 1)
+        def _():
+            far(relay.at[h], h, 1, sem, place(0, 1))
+            wait_slot(near_recv, h, 0, 1)
+            far(slot(h, 0, 1), h, 0, sem, place(2, 0))
+
+        @pl.when(x == 3)
+        def _():
+            near(relay.at[h], h, 0, sem, place(0, 0))
+            far(relay.at[h], h, 0, sem, place(1, 0))
+            pltpu.make_async_copy(detour.at[h], detour.at[h], detour_recv.at[h]).wait()
+            far(detour.at[h], h, 1, sem, place(2, 0))
+
+    def wait_halo(h):
+        wait_slot(near_recv, h, 1, 1)
+
+        @pl.when(x == 0)
+        def _():
+            far(slot(h, 1, 1), h, 1, late_send.at[h], place(1, 0))
+
+        @pl.when(x != 1)
+        def _():
+            wait_slot(near_recv, h, 0, 1)
+
+        for s in range(2):
+            wait_slot(far_recv, h, s, 0)
+
+    def wait_sent(sem, n):
+        ref = keyval.at[0, :, :, pl.ds(0, 128 * n), :]
+        pltpu.make_async_copy(ref, ref, sem).wait()
+
+    def halo_sent(h):
+        @pl.when(x == 0)
+        def _():
+            wait_sent(early_send.at[h], 3)
+            wait_sent(late_send.at[h], 2)
+
+        @pl.when(x == 1)
+        def _():
+            wait_sent(early_send.at[h], 4)
+            wait_sent(late_send.at[h], 2)
+
+        @pl.when(x == 2)
+        def _():
+            wait_sent(early_send.at[h], 4)
+
+        @pl.when(x == 3)
+        def _():
+            wait_sent(early_send.at[h], 2)
+            wait_sent(late_send.at[h], 3)
 
     row_id = lax.broadcasted_iota(jnp.int32, (2 * 128, 128), 0)
     row_id = jnp.where(row_id >= 128, row_id - 128, row_id)
@@ -315,52 +433,74 @@
             device_id=sibling, device_id_type=MESH,
         )
 
-    own_tok.wait()
-    own_q.wait()
-    their_tok.wait()
-    their_q.wait()
-
-    def turn(t, _):
-        @pl.when(t < 4)
-        def _():
-            wait_first(first_recv, t)
-            ring_start(t, 0)
-
-        @pl.when((t >= 1) & (t < 5))
-        def _():
-            ring_wait(t - 1, 1)
-            ring_start(t - 1, 2)
-
-        @pl.when((t >= 2) & (t < 6))
-        def _():
-            ring_wait(t - 2, 3)
-            project(t - 2)
-            halo_copy(t - 2, 0).start()
-
-        @pl.when(t < 4)
-        def _():
-            ring_wait(t, 0)
-            ring_start(t, 1)
-
-        @pl.when((t >= 1) & (t < 5))
-        def _():
-            ring_wait(t - 1, 2)
-            ring_start(t - 1, 3)
-
-        @pl.when((t >= 3) & (t < 7))
-        def _():
-            halo_copy(t - 3, 0).wait_recv()
-            halo_copy(t - 3, 1).start()
-
-        @pl.when(t >= 4)
-        def _():
-            halo_copy(t - 4, 1).wait_recv()
-            attend(t - 4)
-            out_copy(t - 4).start()
-
+
+    def event(e):
+        h, kind_of = rem(e, 4), div(e, 4)
+
+        @pl.when(kind_of == START)
+        def _():
+            first(h)
+
+        @pl.when(kind_of == 0)
+        def _():
+            wait_first(first_recv, h)
+
+        @pl.when((kind_of >= 1) & (kind_of < 4))
+        def _():
+            ring_wait(h, kind_of - 1, False)
+
+        @pl.when(kind_of < 3)
+        def _():
+            ring_start(h, kind_of, False)
+
+        @pl.when(kind_of == 3)
+        def _():
+            ring_start(h, 3, True)
+
+        @pl.when(kind_of == PROJECT)
+        def _():
+            ring_wait(h, 3, True)
+
+            @pl.when(h == 0)
+            def _():
+                own_tok.wait()
+                their_tok.wait()
+
+            project(h)
+            early(h)
+
+        @pl.when(kind_of == LATE)
+        def _():
+            late(h)
+
+        @pl.when(kind_of == ATTEND)
+        def _():
+            wait_halo(h)
+
+            @pl.when(h == 0)
+            def _():
+                own_q.wait()
+                their_q.wait()
+
+            attend(h)
+            out_copy(h).start()
+
+    def group(i, _):
+        word = jnp.int32(0)
+        for k in range(8):
+            coded = 0
+            for e in reversed(ORDER[4 * k : 4 * k + 4]):
+                coded = coded * 32 + e
+            word = jnp.where(i == k, jnp.int32(coded), word)
+
+        def one(_, word):
+            event(rem(word, 32))
+            return div(word, 32)
+
+        lax.fori_loop(0, 4, one, word)
         return 0
 
-    lax.fori_loop(0, 8, turn, 0)
+    lax.fori_loop(0, 8, group, 0)
 
     peak_copy = pltpu.make_async_remote_copy(
         src_ref=peaks.at[core], dst_ref=peaks.at[core], send_sem=peak_sem.at[0],
@@ -385,9 +525,8 @@
         for step in range(4):
             for axis in range(2):
                 for way in range(2):
-                    ring_copy(axis, way, h, step, False).wait_send()
-        halo_copy(h, 0).wait_send()
-        halo_copy(h, 1).wait_send()
+                    ring_copy(axis, way, h, step, False, step == 3).wait_send()
+        halo_sent(h)
         out_copy(h).wait_send()
         theirs = pl.ds(pl.multiple_of((1 - core) * 1024 + h * 256, 256), 256)
         ref = attended.at[:, theirs]
@@ -426,20 +565,24 @@
             jax.ShapeDtypeStruct((6, KVW), f32),
             jax.ShapeDtypeStruct((6, KVW), bf16),
         ),
-        in_specs=[hbm, hbm] + [vmem] * 6,
+        in_specs=[hbm] * 6 + [vmem] * 2,
         out_specs=(vmem,) * 5,
         scratch_shapes=[
             pltpu.VMEM((HEADS, 2, 2, 8, 2, 96, HD), bf16),
             pltpu.VMEM((2, ROWS, WIDTH), bf16),
             pltpu.VMEM((2, ROWS, 1024), bf16),
             pltpu.VMEM((HEADS, 2, 2, 768, HD), bf16),
+            pltpu.VMEM((HEADS, 2, ROWS, HD), bf16),
+            pltpu.VMEM((HEADS, 2, ROWS, HD), bf16),
             pltpu.VMEM((HEADS, ROWS, 256), bf16),
+            pltpu.VMEM((4, 6, KVW), f32),
             pltpu.VMEM((16, 8, 128), f32),
             pltpu.VMEM((16, 8, 128), f32),
             pltpu.VMEM((96, 128), f32),
             pltpu.VMEM((2, HEADS, 2, 8, 128), f32),
             dma((3,)),
             dma((3,)),
+            dma((4,)),
             dma((2,)),
             dma((3,)),
             dma((3,)),
@@ -447,14 +590,18 @@
             dma((2, HEADS)),
             dma((2, 2, HEADS, 4)),
             dma((2, 2, HEADS, 4)),
-            dma((2, HEADS)),
-            dma((2, HEADS)),
+            dma((HEADS,)),
+            dma((HEADS,)),
+            dma((HEADS, 2)),
+            dma((HEADS, 2)),
+            dma((HEADS,)),
+            dma((HEADS,)),
             dma((HEADS,)),
             dma((HEADS,)),
             dma((2,)),
         ],
         compiler_params=pltpu.CompilerParams(
-            collective_id=0, has_side_effects=True, vmem_limit_bytes=40 * 1024 * 1024
+            collective_id=0, has_side_effects=True, vmem_limit_bytes=56 * 1024 * 1024
         ),
     )(tokens[0], queries[0], master, grad, moment, second, cosine, sine)
     return (new_master, new_moment, new_second, codes, attended[None])

time: 172 us -> 119 us (0.69)
  the two profiles are of different devices: /device:TPU:65 before, /device:TPU:3 now
where the time goes in v2:
time: 119 us
  Pallas kernels  109 us (92%)
  local copies, waits for them, and re-layouts  8.1 us (7%)
  other arithmetic  1.39 us (1%)
    pallas_call x1, Pallas kernels, on_device(): pl.pallas_call(kernel, out_shape=(jax.ShapeDtypeStruct((ROWS, KVW), bf16)...  109 us
    unnamed x5, local copies, waits for them, and re-layouts  8.1 us

profile of v2, /device:TPU:3, one launch (start us, length us, event | category | flops | bytes accessed | tf_op | source)
XLA Modules:
  0.0 119.0 jit_solution(16140642723973995020)
XLA Ops:
  0.7 0.5 fusion
  1.2 0.8 pad_maximum_fusion
  2.0 108.9 %shard_map.101 = (bf16[256,2048]{1,0:T(8,128)(2,1)}, f32[6,2048]{1,0:T(8,128)}, f32[6,2048]{1,0:T(8,128)}, f32[6,2048]{1,0:T(8,128)}, bf16[6,2048]{1,0:T(8,128)(2,1)}) custom-call(bf16[256,3072]{1,0:T(8,128)(2,1)} %bitcast.3, bf16[256,2048]{1,0:T(8,128)(2,1)} %bitcast.4, f32[6,2048]{1,0:T(8,128)} %master_hbm.1, f32[6,2048]{1,0:T(8,128)} %grad_hbm.1, ...), custom_call_target="tpu_custom_call" | custom-call | tf_op jit(solution)/shard_map/pallas_call | solution.py:559
  110.9 1.5 %copy.16 = f32[6,2048]{1,0:T(8,128)} copy(f32[6,2048]{1,0:T(8,128)} %get-tuple-element.25) | data formatting | bytes 98304
  112.4 1.5 %copy.17 = f32[6,2048]{1,0:T(8,128)} copy(f32[6,2048]{1,0:T(8,128)} %get-tuple-element.26) | data formatting | bytes 98304
  113.9 1.5 %copy.18 = f32[6,2048]{1,0:T(8,128)} copy(f32[6,2048]{1,0:T(8,128)} %get-tuple-element.27) | data formatting | bytes 98304
  115.3 1.4 %copy.19 = bf16[6,2048]{1,0:T(8,128)(2,1)} copy(bf16[6,2048]{1,0:T(8,128)(2,1)} %get-tuple-element.28) | data formatting | bytes 49152
  116.7 2.3 %copy.20 = bf16[1,256,2048]{2,1,0:T(8,128)(2,1)} copy(bf16[1,256,2048]{2,1,0:T(8,128)(2,1)} %bitcast.5) | data formatting | bytes 2097152
  (2 shorter events, 0.0 us)

commit v3 on v2

--- a/solution.py
+++ b/solution.py
@@ -1,5 +1,3 @@
-import functools
-
 import jax
 import jax.numpy as jnp
 from jax import lax
@@ -25,6 +23,7 @@
 rope_base = 10000.0
 
 MESH = pl.DeviceIdType.MESH
+LIMIT = 52
 HEADS = 4
 LOG2E = 1.4426950408889634
 
@@ -37,9 +36,14 @@
     return [4 * kinds[item[0]] + int(item[1]) for item in text.split()]
 
 
-ORDER = listed("S0 S1 00 S2") + listed("01 S3 10 11") + listed("20 02 21 30")
-ORDER += listed("12 31 P0 03") + listed("22 13 P1 L0") + listed("32 23 P2 L1")
-ORDER += listed("33 A0 P3 L2") + listed("A1 L3 A2 A3")
+ORDER = listed('S0 S1 00 S2')
+ORDER += listed('01 S3 10 11')
+ORDER += listed('20 02 21 30')
+ORDER += listed('12 31 P0 03')
+ORDER += listed('22 13 P1 L0')
+ORDER += listed('32 23 P2 L1')
+ORDER += listed('33 A0 P3 L2')
+ORDER += listed('A1 L3 A2 A3')
 
 
 def rem(a, b):
@@ -51,10 +55,10 @@
 
 
 def kernel(
-    tok_hbm, q_hbm, master_hbm, grad_hbm, moment_hbm, second_hbm, cosine, sine,
-    attended, new_master, new_moment, new_second, codes,
-    weights, tok, qs, keyval, relay, detour, sent_out, state, staged, pieces, block, peaks,
-    tok_sem, q_sem, state_sem, piece_sem, x_send, x_recv, first_send, first_recv,
+    tok_hbm, q_hbm, fresh, cosine, sine,
+    attended, peak_out,
+    along_z, along_y, tok, qs, keyval, relay, detour, sent_out, staged, pieces, block, peaks,
+    tok_sem, q_sem, piece_sem, x_send, x_recv, first_send, first_recv,
     ring_send, ring_recv, early_send, late_send, near_recv, far_recv, relay_recv, detour_recv,
     out_send, out_recv, peak_sem,
 ):
@@ -69,12 +73,6 @@
         return ((rem(zz, 2) * 8 + yy) * 2 + core, div(zz, 2) * 4 + xx)
 
     sibling = (row_group + 1 - core, ctx)
-    loads = [
-        pltpu.make_async_copy(ref, state.at[i], state_sem.at[i])
-        for i, ref in enumerate((master_hbm, grad_hbm, moment_hbm, second_hbm))
-    ]
-    for load in loads:
-        load.start()
     barrier = pltpu.get_barrier_semaphore()
 
     def greet(i, _):
@@ -113,18 +111,6 @@
     own_tok.start()
     own_q.start()
 
-    for load in loads:
-        load.wait()
-    old, g = state[0], state[1]
-    mom = beta_one * state[2] + (1.0 - beta_one) * g
-    sec = beta_two * state[3] + (1.0 - beta_two) * g * g
-    mom_hat = mom / (1.0 - beta_one**step_count)
-    sec_hat = sec / (1.0 - beta_two**step_count)
-    update = mom_hat / (jnp.sqrt(sec_hat) + adam_eps) + decay_rate * old
-    fresh = old - learn_rate * update
-    new_master[...] = fresh
-    new_moment[...] = mom
-    new_second[...] = sec
     staged[...] = jnp.zeros_like(staged)
     for b in range(16):
         staged[b, 0:6, :] = fresh[:, 128 * b : 128 * b + 128]
@@ -161,17 +147,19 @@
 
     for j in range(16):
         block[6 * j : 6 * j + 6, :] = pieces[j, 0:6, :]
-    weights[x, kind, z_lo, y, half] = block[...].astype(jnp.bfloat16)
-
-    def x_copy(k):
-        ref = weights.at[x, kind, z_lo, y, half]
+    along_z[x, z, y] = block[0:48, :].astype(jnp.bfloat16)
+    along_y[x, y, z] = block[48:96, :].astype(jnp.bfloat16)
+
+    def x_copy(k, which):
+        ref = (along_z.at[x, z, y], along_y.at[x, y, z])[which]
         return pltpu.make_async_remote_copy(
-            src_ref=ref, dst_ref=ref, send_sem=x_send.at[k], recv_sem=x_recv.at[k],
+            src_ref=ref, dst_ref=ref, send_sem=x_send.at[which, k], recv_sem=x_recv.at[which, k],
             device_id=device(rem(x + k + 1, 4), y, z), device_id_type=MESH,
         )
 
     for k in range(3):
-        x_copy(k).start()
+        x_copy(k, 0).start()
+        x_copy(k, 1).start()
 
     their_tok = pltpu.make_async_remote_copy(
         src_ref=tok_hbm, dst_ref=tok.at[1], send_sem=tok_sem.at[1], recv_sem=tok_sem.at[2],
@@ -185,12 +173,13 @@
     their_q.start()
 
     for k in range(3):
-        ref = weights.at[rem(x + 3 - k, 4), kind, z_lo, y, half]
-        pltpu.make_async_copy(ref, ref, x_recv.at[k]).wait()
+        origin = rem(x + 3 - k, 4)
+        for which, ref in enumerate((along_z.at[origin, z, y], along_y.at[origin, y, z])):
+            pltpu.make_async_copy(ref, ref, x_recv.at[which, k]).wait()
 
     def first(h):
-        upper = weights.at[h, kind, z_lo, y, half, pl.ds(0, 48), :]
-        lower = weights.at[h, kind, z_lo, y, half, pl.ds(48, 48), :]
+        upper = along_z.at[h, z, y]
+        lower = along_y.at[h, y, z]
 
         def to_peer(k, _):
             pltpu.make_async_remote_copy(
@@ -209,17 +198,11 @@
 
     def wait_first(sems, h):
         for axis in range(2):
-            ref = weights.at[h, 0, 0, pl.ds(0, 7), 0, pl.ds(0, 48), :]
+            ref = along_z.at[h, 0, pl.ds(0, 7)]
             pltpu.make_async_copy(ref, ref, sems.at[axis, h]).wait()
 
     def part(axis, h, at, which):
-        if axis == 0:
-            rows = (pl.ds(0, 8), pl.ds(0, 4), pl.ds(4, 4))[which]
-            return weights.at[
-                h, div(at, 4), rem(at, 2), rows, rem(div(at, 2), 2), pl.ds(0, 48), :
-            ]
-        kinds = (pl.ds(0, 2), pl.ds(0, 1), pl.ds(1, 1))[which]
-        return weights.at[h, kinds, :, at, :, pl.ds(48, 48), :]
+        return (along_z, along_y)[axis].at[h, at, (pl.ds(0, 8), pl.ds(0, 4), pl.ds(4, 4))[which]]
 
     def ring_copy(axis, way, h, step, received, last):
         here = (z, y)[axis]
@@ -249,9 +232,14 @@
         total = jnp.zeros((2 * ROWS, 2 * HD), jnp.float32)
         top = jnp.zeros((8, 2 * HD), jnp.float32)
         for c in range(4):
-            low = weights[h, 0, c // 2, 4 * (c % 2) : 4 * (c % 2) + 4].reshape(768, HD)
-            high = weights[h, 1, c // 2, 4 * (c % 2) : 4 * (c % 2) + 4].reshape(768, HD)
-            both = jnp.concatenate([low, high], axis=1)
+            sides = []
+            for kv in range(2):
+                strips = []
+                for yy in range(4 * (c % 2), 4 * (c % 2) + 4):
+                    for zz in (4 * kv + c // 2, 4 * kv + 2 + c // 2):
+                        strips += [along_z[h, zz, yy], along_y[h, yy, zz]]
+                sides.append(jnp.concatenate(strips, axis=0))
+            both = jnp.concatenate(sides, axis=1)
             rows = tok[:, :, 768 * c : 768 * c + 768].reshape(2 * ROWS, 768)
             total = total + jnp.dot(rows, both, preferred_element_type=jnp.float32)
             size = jnp.abs(both.astype(jnp.float32)).reshape(96, 8, 2 * HD)
@@ -518,7 +506,8 @@
         pltpu.make_async_copy(staged, staged, piece_sem.at[0]).wait()
 
     for k in range(3):
-        x_copy(k).wait_send()
+        x_copy(k, 0).wait_send()
+        x_copy(k, 1).wait_send()
 
     def drain(h, _):
         wait_first(first_send, h)
@@ -540,11 +529,20 @@
     pltpu.make_async_copy(ref, ref, peak_sem.at[1]).wait()
     for b in range(16):
         head = b % 8
-        peak = peaks[head // 4, head % 4, b // 8, 0:1, :] + 1e-06
-        codes[:, 128 * b : 128 * b + 128] = (staged[b, 0:6, :] / peak).astype(jnp.bfloat16)
+        peak_out[:, 128 * b : 128 * b + 128] = peaks[head // 4, head % 4, b // 8, 0:1, :] + 1e-06
+
+
+def adamw(master, grad, moment, second):
+    new_moment = beta_one * moment + (1.0 - beta_one) * grad
+    new_second = beta_two * second + (1.0 - beta_two) * grad * grad
+    moment_hat = new_moment / (1.0 - beta_one**step_count)
+    second_hat = new_second / (1.0 - beta_two**step_count)
+    update = moment_hat / (jnp.sqrt(second_hat) + adam_eps) + decay_rate * master
+    return (master - learn_rate * update, new_moment, new_second)
 
 
 def on_device(tokens, queries, master, grad, moment, second):
+    new_master, new_moment, new_second = adamw(master, grad, moment, second)
     query_start = lax.axis_index("ctx") * ROWS
     positions = query_start + jnp.arange(ROWS, dtype=jnp.int32)
     freqs = rope_base ** (-jnp.arange(HD // 2, dtype=jnp.float32) * 2.0 / HD)
@@ -556,36 +554,32 @@
     hbm = pl.BlockSpec(memory_space=pl.ANY)
     dma = pltpu.SemaphoreType.DMA
     f32, bf16 = jnp.float32, jnp.bfloat16
-    attended, new_master, new_moment, new_second, codes = pl.pallas_call(
+    attended, peak = pl.pallas_call(
         kernel,
         out_shape=(
             jax.ShapeDtypeStruct((ROWS, KVW), bf16),
-            jax.ShapeDtypeStruct((6, KVW), f32),
-            jax.ShapeDtypeStruct((6, KVW), f32),
-            jax.ShapeDtypeStruct((6, KVW), f32),
-            jax.ShapeDtypeStruct((6, KVW), bf16),
+            jax.ShapeDtypeStruct((1, KVW), f32),
         ),
-        in_specs=[hbm] * 6 + [vmem] * 2,
-        out_specs=(vmem,) * 5,
+        in_specs=[hbm] * 2 + [vmem] * 3,
+        out_specs=(vmem,) * 2,
         scratch_shapes=[
-            pltpu.VMEM((HEADS, 2, 2, 8, 2, 96, HD), bf16),
+            pltpu.VMEM((HEADS, 8, 8, 48, HD), bf16),
+            pltpu.VMEM((HEADS, 8, 8, 48, HD), bf16),
             pltpu.VMEM((2, ROWS, WIDTH), bf16),
             pltpu.VMEM((2, ROWS, 1024), bf16),
             pltpu.VMEM((HEADS, 2, 2, 768, HD), bf16),
             pltpu.VMEM((HEADS, 2, ROWS, HD), bf16),
             pltpu.VMEM((HEADS, 2, ROWS, HD), bf16),
             pltpu.VMEM((HEADS, ROWS, 256), bf16),
-            pltpu.VMEM((4, 6, KVW), f32),
             pltpu.VMEM((16, 8, 128), f32),
             pltpu.VMEM((16, 8, 128), f32),
             pltpu.VMEM((96, 128), f32),
             pltpu.VMEM((2, HEADS, 2, 8, 128), f32),
             dma((3,)),
             dma((3,)),
-            dma((4,)),
             dma((2,)),
-            dma((3,)),
-            dma((3,)),
+            dma((2, 3)),
+            dma((2, 3)),
             dma((2, HEADS)),
             dma((2, HEADS)),
             dma((2, 2, HEADS, 4)),
@@ -601,9 +595,10 @@
             dma((2,)),
         ],
         compiler_params=pltpu.CompilerParams(
-            collective_id=0, has_side_effects=True, vmem_limit_bytes=56 * 1024 * 1024
+            collective_id=0, has_side_effects=True, vmem_limit_bytes=LIMIT * 1024 * 1024
         ),
-    )(tokens[0], queries[0], master, grad, moment, second, cosine, sine)
+    )(tokens[0], queries[0], new_master, cosine, sine)
+    codes = (new_master / peak).astype(bf16)
     return (new_master, new_moment, new_second, codes, attended[None])
 
 

time: 119 us -> 110 us (0.924)
  local copies, waits for them, and re-layouts: 8.1 us -> 0.97 us
  Pallas kernels: 109 us -> 105 us
  other arithmetic: 1.39 us -> 2.94 us
    unnamed x5 -> x3, local copies, waits for them, and re-layouts: 8.1 us -> 0.97 us
    pallas_call x1, Pallas kernels: 109 us -> 105 us  [on_device(): pl.pallas_call(kernel, out_shape=(jax.ShapeDtypeStruct((ROWS, KVW), bf16)...]
    sub x0 -> x1, other arithmetic: none -> 1.63 us  [adamw(): return (master - learn_rate * update, new_moment, new_second)]
where the time goes in v3:
time: 110 us
  Pallas kernels  105 us (95%)
  other arithmetic  2.94 us (3%)
    pallas_call x1, Pallas kernels, on_device(): pl.pallas_call(kernel, out_shape=(jax.ShapeDtypeStruct((ROWS, KVW), bf16)...  105 us

profile of v3, /device:TPU:3, one launch (start us, length us, event | category | flops | bytes accessed | tf_op | source)
XLA Modules:
  0.0 109.9 jit_solution(18358082735954324430)
XLA Ops:
  0.7 1.6 %multiply_subtract_fusion = (f32[6,2048]{1,0:T(8,128)S(1)}, f32[6,2048]{1,0:T(8,128)}, f32[6,2048]{1,0:T(8,128)}) fusion(f32[6,2048]{1,0:T(8,128)} %param.8, f32[6,2048]{1,0:T(8,128)} %param.9, f32[6,2048]{1,0:T(8,128)} %param.11, f32[6,2048]{1,0:T(8,128)} %param.10), kind=kLoop, calls=%fused_computation.7 | loop fusion | flops 159744 | bytes 344064 | tf_op jit(solution)/shard_map/sub | solution.py:541
  2.3 0.0 copy-start
  2.3 0.5 fusion.1
  2.8 0.1 pad_maximum_fusion
  3.0 105.3 %shard_map.101 = (bf16[256,2048]{1,0:T(8,128)(2,1)S(1)}, f32[1,2048]{1,0:T(1,128)S(1)}) custom-call(bf16[256,3072]{1,0:T(8,128)(2,1)} %bitcast.6, bf16[256,2048]{1,0:T(8,128)(2,1)} %bitcast.7, f32[6,2048]{1,0:T(8,128)S(1)} %get-tuple-element.22.fresh, f32[256,128]{1,0:T(8,128)S(1)} %get-tuple-element.15.cosine, f32[256,128]{1,0:T(8,128)S(1)} %get-tuple-element.16.sine), custom_call_target="tpu_custom_call" | custom-call | tf_op jit(solution)/shard_map/pallas_call | solution.py:557
  108.2 0.0 copy-done
  108.3 0.6 divide_convert_fusion
  108.9 1.0 copy.12
  (2 shorter events, 0.0 us)
Async XLA Ops:
  2.3 106.0 %copy-start = (f32[6,2048]{1,0:T(8,128)}, f32[6,2048]{1,0:T(8,128)S(1)}, u32[]{:S(2)}) copy-start(f32[6,2048]{1,0:T(8,128)S(1)} %get-tuple-element.22.fresh) | copy-start | bytes 147460

commit v4 on v3

--- a/solution.py
+++ b/solution.py
@@ -221,6 +221,12 @@
     def ring_start(h, step, last):
         for axis in range(2):
             for way in range(2):
+                ring_copy(axis, way, h, step, False, last).start()
+
+    def ring_pass(h, step, last):
+        for axis in range(2):
+            for way in range(2):
+                ring_copy(axis, way, h, step - 1, True, False).wait_recv()
                 ring_copy(axis, way, h, step, False, last).start()
 
     def ring_wait(h, step, last):
@@ -314,6 +320,10 @@
         def _():
             near(relay.at[h], h, 1, sem, place(0, 1))
 
+            @pl.when(h == 3)
+            def _():
+                far(relay.at[h], h, 1, sem, place(1, 1))
+
         @pl.when(x == 1)
         def _():
             far(relay.at[h], h, 1, sem, place(0, 1))
@@ -330,7 +340,7 @@
     def wait_halo(h):
         wait_slot(near_recv, h, 1, 1)
 
-        @pl.when(x == 0)
+        @pl.when((x == 0) & (h < 3))
         def _():
             far(slot(h, 1, 1), h, 1, late_send.at[h], place(1, 0))
 
@@ -372,7 +382,7 @@
 
     def attend(h):
         def one(i, _):
-            s, a = div(i, 2), rem(i, 2)
+            s, a = 1 - div(i, 2), rem(i, 2)
             start = pl.multiple_of(a * 128, 128)
             cols = pl.ds(pl.multiple_of(h * 256, 256), 256)
             q = qs[s, pl.ds(start, 128), cols]
@@ -409,6 +419,10 @@
             def _():
                 sent_out[h, pl.ds(start, 128), :] = mixed
 
+            @pl.when(i == 1)
+            def _():
+                out_copy(h).start()
+
             return 0
 
         lax.fori_loop(0, 4, one, 0)
@@ -422,6 +436,11 @@
         )
 
 
+    peak_copy = pltpu.make_async_remote_copy(
+        src_ref=peaks.at[core], dst_ref=peaks.at[core], send_sem=peak_sem.at[0],
+        recv_sem=peak_sem.at[1], device_id=sibling, device_id_type=MESH,
+    )
+
     def event(e):
         h, kind_of = rem(e, 4), div(e, 4)
 
@@ -433,17 +452,17 @@
         def _():
             wait_first(first_recv, h)
 
-        @pl.when((kind_of >= 1) & (kind_of < 4))
-        def _():
-            ring_wait(h, kind_of - 1, False)
-
-        @pl.when(kind_of < 3)
-        def _():
-            ring_start(h, kind_of, False)
+        @pl.when(kind_of == 0)
+        def _():
+            ring_start(h, 0, False)
+
+        @pl.when((kind_of >= 1) & (kind_of < 3))
+        def _():
+            ring_pass(h, kind_of, False)
 
         @pl.when(kind_of == 3)
         def _():
-            ring_start(h, 3, True)
+            ring_pass(h, 3, True)
 
         @pl.when(kind_of == PROJECT)
         def _():
@@ -457,6 +476,10 @@
             project(h)
             early(h)
 
+            @pl.when(h == 3)
+            def _():
+                peak_copy.start()
+
         @pl.when(kind_of == LATE)
         def _():
             late(h)
@@ -471,7 +494,6 @@
                 their_q.wait()
 
             attend(h)
-            out_copy(h).start()
 
     def group(i, _):
         word = jnp.int32(0)
@@ -490,11 +512,6 @@
 
     lax.fori_loop(0, 8, group, 0)
 
-    peak_copy = pltpu.make_async_remote_copy(
-        src_ref=peaks.at[core], dst_ref=peaks.at[core], send_sem=peak_sem.at[0],
-        recv_sem=peak_sem.at[1], device_id=sibling, device_id_type=MESH,
-    )
-    peak_copy.start()
 
     @pl.when(half == core)
     def _():

time: 110 us -> 109 us (level)
  the two profiles are of different devices: /device:TPU:3 before, /device:TPU:11 now
where the time goes in v4:
time: 109 us
  Pallas kernels  105 us (96%)
  other arithmetic  2.94 us (3%)
    pallas_call x1, Pallas kernels, on_device(): pl.pallas_call(kernel, out_shape=(jax.ShapeDtypeStruct((ROWS, KVW), bf16)...  105 us

profile of v4, /device:TPU:11, one launch (start us, length us, event | category | flops | bytes accessed | tf_op | source)
XLA Modules:
  0.0 109.1 jit_solution(4764649770692542456)
XLA Ops:
  0.7 1.6 %multiply_subtract_fusion = (f32[6,2048]{1,0:T(8,128)S(1)}, f32[6,2048]{1,0:T(8,128)}, f32[6,2048]{1,0:T(8,128)}) fusion(f32[6,2048]{1,0:T(8,128)} %param.8, f32[6,2048]{1,0:T(8,128)} %param.9, f32[6,2048]{1,0:T(8,128)} %param.11, f32[6,2048]{1,0:T(8,128)} %param.10), kind=kLoop, calls=%fused_computation.7 | loop fusion | flops 159744 | bytes 344064 | tf_op jit(solution)/shard_map/sub | solution.py:558
  2.3 0.0 copy-start
  2.3 0.5 fusion.1
  2.8 0.1 pad_maximum_fusion
  3.0 104.5 %shard_map.101 = (bf16[256,2048]{1,0:T(8,128)(2,1)S(1)}, f32[1,2048]{1,0:T(1,128)S(1)}) custom-call(bf16[256,3072]{1,0:T(8,128)(2,1)} %bitcast.6, bf16[256,2048]{1,0:T(8,128)(2,1)} %bitcast.7, f32[6,2048]{1,0:T(8,128)S(1)} %get-tuple-element.22.fresh, f32[256,128]{1,0:T(8,128)S(1)} %get-tuple-element.15.cosine, f32[256,128]{1,0:T(8,128)S(1)} %get-tuple-element.16.sine), custom_call_target="tpu_custom_call" | custom-call | tf_op jit(solution)/shard_map/pallas_call | solution.py:574
  107.5 0.0 copy-done
  107.5 0.6 divide_convert_fusion
  108.1 1.0 copy.12
  (2 shorter events, 0.0 us)
Async XLA Ops:
  2.3 105.2 %copy-start = (f32[6,2048]{1,0:T(8,128)}, f32[6,2048]{1,0:T(8,128)S(1)}, u32[]{:S(2)}) copy-start(f32[6,2048]{1,0:T(8,128)S(1)} %get-tuple-element.22.fresh) | copy-start | bytes 147460

commit v5 on v4

--- a/solution.py
+++ b/solution.py
@@ -39,8 +39,8 @@
 ORDER = listed('S0 S1 00 S2')
 ORDER += listed('01 S3 10 11')
 ORDER += listed('20 02 21 30')
-ORDER += listed('12 31 P0 03')
-ORDER += listed('22 13 P1 L0')
+ORDER += listed('12 P0 31 03')
+ORDER += listed('22 L0 P1 13')
 ORDER += listed('32 23 P2 L1')
 ORDER += listed('33 A0 P3 L2')
 ORDER += listed('A1 L3 A2 A3')

time: 109 us -> 114 us (1.046)
  the two profiles are of different devices: /device:TPU:11 before, /device:TPU:131 now
where the time goes in v5:
time: 114 us
  Pallas kernels  110 us (96%)
  other arithmetic  2.94 us (3%)
    pallas_call x1, Pallas kernels, on_device(): pl.pallas_call(kernel, out_shape=(jax.ShapeDtypeStruct((ROWS, KVW), bf16)...  110 us

profile of v5, /device:TPU:131, one launch (start us, length us, event | category | flops | bytes accessed | tf_op | source)
XLA Modules:
  0.0 114.1 jit_solution(17912007937300439146)
XLA Ops:
  0.7 1.6 %multiply_subtract_fusion = (f32[6,2048]{1,0:T(8,128)S(1)}, f32[6,2048]{1,0:T(8,128)}, f32[6,2048]{1,0:T(8,128)}) fusion(f32[6,2048]{1,0:T(8,128)} %param.8, f32[6,2048]{1,0:T(8,128)} %param.9, f32[6,2048]{1,0:T(8,128)} %param.11, f32[6,2048]{1,0:T(8,128)} %param.10), kind=kLoop, calls=%fused_computation.7 | loop fusion | flops 159744 | bytes 344064 | tf_op jit(solution)/shard_map/sub | solution.py:558
  2.3 0.0 copy-start
  2.3 0.5 fusion.1
  2.8 0.1 pad_maximum_fusion
  3.0 109.5 %shard_map.101 = (bf16[256,2048]{1,0:T(8,128)(2,1)S(1)}, f32[1,2048]{1,0:T(1,128)S(1)}) custom-call(bf16[256,3072]{1,0:T(8,128)(2,1)} %bitcast.6, bf16[256,2048]{1,0:T(8,128)(2,1)} %bitcast.7, f32[6,2048]{1,0:T(8,128)S(1)} %get-tuple-element.22.fresh, f32[256,128]{1,0:T(8,128)S(1)} %get-tuple-element.15.cosine, f32[256,128]{1,0:T(8,128)S(1)} %get-tuple-element.16.sine), custom_call_target="tpu_custom_call" | custom-call | tf_op jit(solution)/shard_map/pallas_call | solution.py:574
  112.5 0.0 copy-done
  112.5 0.6 divide_convert_fusion
  113.2 1.0 copy.12
  (2 shorter events, 0.0 us)
Async XLA Ops:
  2.3 110.2 %copy-start = (f32[6,2048]{1,0:T(8,128)}, f32[6,2048]{1,0:T(8,128)S(1)}, u32[]{:S(2)}) copy-start(f32[6,2048]{1,0:T(8,128)S(1)} %get-tuple-element.22.fresh) | copy-start | bytes 147460
